TPU v7x, 32 devices: a whole 2x2x4 slice. The times are simulated.
32 devices in a mesh: grp: 2 (over x), basis: 16 (over z, y, core).
Axes of the slice: x: 2, y: 2, z: 4, core: 2. Of those that a mesh axis runs over, the one named last changes fastest.
Arguments:
- query_inputs: bfloat16 [384, 4096], P(('grp', 'basis')), parts along dimension 0, may hold values from -6 to 6
- query_grads: bfloat16 [384, 14336], P(('grp', 'basis')), parts along dimension 0, may hold values from -6 to 6
- basis_in: bfloat16 [4096, 4096], P(None, 'basis'), may hold values from -0.09375 to 0.09375
- basis_out: bfloat16 [14336, 14336], P(None, 'basis'), may hold values from -0.046875 to 0.046875
- eig_in: float32 [4096], P('basis'), may hold values from 0.01 to 10
- eig_out: float32 [14336], P('basis'), may hold values from 0.01 to 10
- trace_inputs: bfloat16 [4096, 4096], P(('grp', 'basis')), parts along dimension 0, may hold values from -6 to 6
- trace_grads: bfloat16 [4096, 14336], P(('grp', 'basis')), parts along dimension 0, may hold values from -6 to 6
Outputs:
- scores: float32 [64, 64], P(None, ('grp', 'basis')), parts along dimension 1
There are 2 independent parts, one for each index of `grp`. A program takes and returns all parts, laid end to end along the dimension named above; an argument that names none is the same for every part. Nothing has to cross between parts.
All inputs are finite; a program needn't handle non-finite values.
Results may differ from a plain program's by a relative error of at most 0.0075.
Values may be sent and summed in bfloat16 or wider, within the bound.
A program may use at most 128 MiB of HBM per device.

v0:
```python
import math

import jax
import jax.numpy as jnp
from jax import lax
from jax.sharding import PartitionSpec as P

DA = 4096
FW = 14336
QUERIES = 64
QTOK = 3
TTOK = 64


damping = 0.1


def per_device(
    query_inputs, query_grads, basis_in, basis_out, eig_in, eig_out, trace_inputs, trace_grads
):
    full_in, full_grad = (
        lax.all_gather(query_inputs, "basis", axis=0, tiled=True),
        lax.all_gather(query_grads, "basis", axis=0, tiled=True),
    )
    rot_in = (
        jnp.dot(full_in, basis_in, preferred_element_type=jnp.float32) / (eig_in + damping)
    ).astype(jnp.bfloat16)
    rot_grad = (
        jnp.dot(full_grad, basis_out, preferred_element_type=jnp.float32) / (eig_out + damping)
    ).astype(jnp.bfloat16)
    block = basis_in
    share_in = lax.psum_scatter(
        jnp.dot(block, rot_in.T, preferred_element_type=jnp.float32),
        "basis",
        scatter_dimension=0,
        tiled=True,
    )
    block = basis_out
    share_grad = lax.psum_scatter(
        jnp.dot(block, rot_grad.T, preferred_element_type=jnp.float32),
        "basis",
        scatter_dimension=0,
        tiled=True,
    )
    pre_in, pre_grad = (
        lax.all_gather(share_in.astype(jnp.bfloat16), "basis", axis=0, tiled=True).astype(
            share_in.dtype
        ),
        lax.all_gather(share_grad.astype(jnp.bfloat16), "basis", axis=0, tiled=True).astype(
            share_grad.dtype
        ),
    )
    pair_in = jnp.dot(
        trace_inputs.astype(jnp.float32), pre_in, precision=lax.Precision.HIGHEST
    ) / math.sqrt(DA)
    pair_grad = jnp.dot(
        trace_grads.astype(jnp.float32), pre_grad, precision=lax.Precision.HIGHEST
    ) / math.sqrt(FW)
    local_traces = trace_inputs.shape[0] // TTOK
    products = (pair_in * pair_grad).reshape(local_traces, TTOK, QUERIES, QTOK)
    return jnp.sum(products, axis=(1, 3)).T / (TTOK * QTOK)


def solution(mesh):
    return jax.shard_map(
        per_device,
        mesh=mesh,
        in_specs=(
            P(("grp", "basis"), None),
            P(("grp", "basis"), None),
            P(None, "basis"),
            P(None, "basis"),
            P("basis"),
            P("basis"),
            P(("grp", "basis"), None),
            P(("grp", "basis"), None),
        ),
        out_specs=P(None, ("grp", "basis")),
        check_vma=False,
    )
```

profile of v0, /device:TPU:1, one launch (start us, length us, event | category | flops | bytes accessed | tf_op | source)
XLA Modules:
  0.0 430.2 jit_solution(14910716109502090666)
XLA Ops:
  6.5 0.0 copy-start
  6.5 0.0 all-gather.11.cloned.1.call-start
  6.5 0.7 all-gather.11.cloned.1.call-update
  7.3 0.0 all-gather.13.cloned.1.call-start
  7.3 0.7 all-gather.13.cloned.1.call-update
  8.0 0.0 reduce-scatter.3.cloned.1.call-start
  8.1 0.7 broadcast_add_fusion.1
  8.7 0.7 broadcast_add_fusion
  9.4 44.0 %all-gather.11.cloned.1.call-done = bf16[16,12,4096]{2,1,0:T(8,128)(2,1)} async-done(((bf16[1,12,4096]{2,1,0:T(8,128)(2,1)}), bf16[16,12,4096]{2,1,0:T(8,128)(2,1)}) %all-gather.11.cloned.1.call-update) | async-done | bytes 1572880 | tf_op jit(solution)/shard_map/all_gather | solution.py:22
  53.5 3.6 reshape.7
  57.0 0.0 copy-done
  57.0 5.1 %convolution_bitcast_fusion.1 = f32[4096,192]{0,1:T(8,128)} fusion(bf16[4096,256]{1,0:T(8,128)(2,1)S(1)} %copy-done, bf16[192,4096]{1,0:T(8,128)(2,1)} %reshape.7, f32[256]{0:T(256)S(1)} %broadcast_add_fusion.1), kind=kOutput, calls=%fused_computation.1 | convolution fusion | flops 805404672 | bytes 6816768 | tf_op jit(solution)/shard_map/dot_general | solution.py:33
  62.1 0.0 reduce-scatter.3.cloned.1.call-update
  62.1 0.0 reduce-scatter.5.cloned.1.call-start
  62.2 60.7 %all-gather.13.cloned.1.call-done = bf16[16,12,14336]{2,1,0:T(8,128)(2,1)} async-done(((bf16[1,12,14336]{2,1,0:T(8,128)(2,1)}), bf16[16,12,14336]{2,1,0:T(8,128)(2,1)}) %all-gather.13.cloned.1.call-update) | async-done | bytes 5505040 | tf_op jit(solution)/shard_map/all_gather | solution.py:23
  122.8 8.3 %reshape.9 = bf16[192,14336]{1,0:T(8,128)(2,1)} reshape(bf16[16,12,14336]{2,1,0:T(8,128)(2,1)} %all-gather.13.cloned.1.call-done) | data formatting | bytes 11010048
  131.1 14.2 %fusion = bf16[192,896]{1,0:T(8,128)(2,1)S(1)} fusion(bf16[192,14336]{1,0:T(8,128)(2,1)} %reshape.9, bf16[14336,896]{1,0:T(8,128)(2,1)} %param.11, f32[896]{0:T(1024)S(1)} %broadcast_add_fusion), kind=kOutput, calls=%fused_computation.3 | convolution fusion | flops 4932845568 | bytes 31542784 | tf_op jit(solution)/shard_map/dot_general | solution.py:29
  145.3 15.9 %convolution_bitcast_fusion = f32[14336,192]{0,1:T(8,128)} fusion(bf16[192,896]{1,0:T(8,128)(2,1)S(1)} %fusion, bf16[14336,896]{1,0:T(8,128)(2,1)} %param.11), kind=kOutput, calls=%fused_computation | convolution fusion | flops 4932501504 | bytes 37044224 | tf_op jit(solution)/shard_map/dot_general | solution.py:40
  161.2 0.0 copy-start.2
  161.2 0.0 reduce-scatter.5.cloned.1.call-update
  161.2 0.0 all-gather.7.cloned.1.call-start
  161.3 28.3 %reduce-scatter.3.cloned.1.call-done = f32[256,192]{0,1:T(8,128)} async-done(((f32[4096,192]{0,1:T(8,128)}), f32[256,192]{0,1:T(8,128)}) %reduce-scatter.3.cloned.1.call-update) | async-done | bytes 196624 | tf_op jit(solution)/shard_map/reduce_scatter | solution.py:32
  189.6 1.6 convert_element_type.17
  191.2 0.0 all-gather.7.cloned.1.call-update
  191.2 0.0 all-gather.9.cloned.1.call-start
  191.3 125.1 %reduce-scatter.5.cloned.1.call-done = f32[896,192]{0,1:T(8,128)} async-done(((f32[14336,192]{0,1:T(8,128)}), f32[896,192]{0,1:T(8,128)}) %reduce-scatter.5.cloned.1.call-update) | async-done | bytes 688144 | tf_op jit(solution)/shard_map/reduce_scatter | solution.py:39
  316.3 1.9 convert_element_type.19
  318.2 0.0 all-gather.9.cloned.1.call-update
  318.2 39.7 %all-gather.7.cloned.1.call-done = bf16[4096,192]{0,1:T(8,128)(2,1)} async-done(((bf16[256,192]{0,1:T(8,128)(2,1)}), bf16[4096,192]{0,1:T(8,128)(2,1)}) %all-gather.7.cloned.1.call-update) | async-done | bytes 1572880 | tf_op jit(solution)/shard_map/all_gather | solution.py:46
  357.9 0.0 copy-done.2
  357.9 0.0 copy-start.1
  357.9 2.1 convolution_multiply_fusion.1
  360.1 57.0 %all-gather.9.cloned.1.call-done = bf16[14336,192]{0,1:T(8,128)(2,1)} async-done(((bf16[896,192]{0,1:T(8,128)(2,1)}), bf16[14336,192]{0,1:T(8,128)(2,1)}) %all-gather.9.cloned.1.call-update) | async-done | bytes 5505040 | tf_op jit(solution)/shard_map/all_gather | solution.py:49
  417.1 5.2 %fusion.3 = f32[128,192]{0,1:T(8,128)S(1)} fusion(f32[192,128]{1,0:T(8,128)S(1)} %convolution_multiply_fusion.1, bf16[14336,192]{0,1:T(8,128)(2,1)} %all-gather.9.cloned.1.call-done, bf16[128,14336]{1,0:T(8,128)(2,1)} %param.15), kind=kOutput, calls=%fused_computation.8 | convolution fusion | flops 704692224 | bytes 9371648 | tf_op jit(solution)/shard_map/dot_general | solution.py:56
  422.4 0.2 reshape.5
  422.5 0.2 reduce_sum.9
  422.7 0.6 copy.9
  423.3 0.0 copy-done.1
  (1 shorter events, 0.0 us)
Async XLA Ops:
  6.5 50.5 %copy-start = (bf16[4096,256]{1,0:T(8,128)(2,1)S(1)}, bf16[4096,256]{1,0:T(8,128)(2,1)}, u32[]{:S(2)}) copy-start(bf16[4096,256]{1,0:T(8,128)(2,1)} %param.10) | copy-start | bytes 6291460
  6.5 46.9 %all-gather.11.cloned.1.call-start = ((), (), s32[]{:S(2)}) async-start(), calls=%async_computation.6 | async-start | bytes 2228224 | tf_op jit(solution)/shard_map/all_gather | solution.py:22
  7.3 115.6 %all-gather.13.cloned.1.call-start = ((), (), s32[]{:S(2)}) async-start(), calls=%async_computation.7 | async-start | bytes 7798784 | tf_op jit(solution)/shard_map/all_gather | solution.py:23
  8.0 181.6 %reduce-scatter.3.cloned.1.call-start = ((), (), s32[]{:S(2)}) async-start(), calls=%async_computation.2 | async-start | bytes 3342336 | tf_op jit(solution)/shard_map/reduce_scatter | solution.py:32
  62.1 254.2 %reduce-scatter.5.cloned.1.call-start = ((), (), s32[]{:S(2)}) async-start(), calls=%async_computation.4 | async-start | bytes 11698176 | tf_op jit(solution)/shard_map/reduce_scatter | solution.py:39
  161.2 196.7 %copy-start.2 = (bf16[128,4096]{1,0:T(8,128)(2,1)S(1)}, bf16[128,4096]{1,0:T(8,128)(2,1)}, u32[]{:S(2)}) copy-start(bf16[128,4096]{1,0:T(8,128)(2,1)} %param.14) | copy-start | bytes 3145732
  161.2 196.7 %all-gather.7.cloned.1.call-start = ((), (), s32[]{:S(2)}) async-start(), calls=%async_computation.3 | async-start | bytes 1671168 | tf_op jit(solution)/shard_map/all_gather | solution.py:46
  191.2 225.9 %all-gather.9.cloned.1.call-start = ((), (), s32[]{:S(2)}) async-start(), calls=%async_computation.5 | async-start | bytes 5849088 | tf_op jit(solution)/shard_map/all_gather | solution.py:49
  357.9 65.4 %copy-start.1 = (bf16[4096,256]{1,0:T(8,128)(2,1)S(1)}, bf16[4096,256]{1,0:T(8,128)(2,1)}, u32[]{:S(2)}) copy-start(bf16[4096,256]{1,0:T(8,128)(2,1)} %param.10) | copy-start | bytes 6291460
Sparse Core Ops, SparseCore 0:
  9.5 43.8 all-gather.10
  55.7 67.0 all-gather.12
  126.6 62.9 reduce-scatter.2
  193.6 122.7 reduce-scatter.4
  318.6 39.3 all-gather.6
  360.2 56.8 all-gather.8
where the time goes:
time: 431 us; the launch traced here: 430 us
  waiting for transfers between devices  356 us (83%)
  matrix products  42.5 us (10%)
  between operations  13.5 us (3%)
  local copies, waits for them, and re-layouts  12.7 us (3%)
  other arithmetic  4.96 us (1%)
    reduce_scatter x1, waiting for transfers between devices, per_device(): lax.psum_scatter(jnp.dot(block, rot_grad.T, preferred_element_type=jnp.fl...  125 us
    all_gather x1, waiting for transfers between devices, per_device(): lax.all_gather(query_grads, 'basis', axis=0, tiled=True)  60.7 us
    all_gather x1, waiting for transfers between devices, per_device(): lax.all_gather(share_grad.astype(jnp.bfloat16), 'basis', axis=0, tiled=True)  57 us
    all_gather x1, waiting for transfers between devices, per_device(): lax.all_gather(query_inputs, 'basis', axis=0, tiled=True)  44 us
    all_gather x1, waiting for transfers between devices, per_device(): lax.all_gather(share_in.astype(jnp.bfloat16), 'basis', axis=0, tiled=True)  39.7 us
    reduce_scatter x1, waiting for transfers between devices, per_device(): lax.psum_scatter(jnp.dot(block, rot_in.T, preferred_element_type=jnp.floa...  28.3 us
    dot_general x1, matrix products, per_device(): jnp.dot(block, rot_grad.T, preferred_element_type=jnp.float32)  15.9 us
    dot_general x1, matrix products, per_device(): jnp.dot(full_grad, basis_out, preferred_element_type=jnp.float32)  14.2 us
  transfers between devices with their start and end apart: 6, of which 6 were waited for; matrix products, arithmetic and copies ran while one was open for 13% of the time, Pallas kernels for 0%

commit v1 on v0

v1 whole, which is shorter than its diff:
```python
import functools
import math

import jax
import jax.numpy as jnp
from jax import lax
from jax.experimental import pallas as pl
from jax.experimental.pallas import tpu as pltpu
from jax.sharding import PartitionSpec as P

DA = 4096
FW = 14336
QUERIES = 64
QTOK = 3
TTOK = 64
QROWS = QUERIES * QTOK
FEAT = DA + FW
CHIPS = 8
CORES = 2
HOPS = CHIPS // 2
PAD = 16
ROWS = QROWS // (CHIPS * CORES)
IN_HALF, OUT_HALF = DA // CORES, FW // CORES
HALF = IN_HALF + OUT_HALF
IN_CHUNK, OUT_CHUNK = IN_HALF // CHIPS, OUT_HALF // CHIPS
CHUNK = IN_CHUNK + OUT_CHUNK
KTILE = 1024

damping = 0.1
F32 = jnp.float32
BF16 = jnp.bfloat16


def nt(a, b):
    return lax.dot_general(a, b, (((1,), (1,)), ((), ())), preferred_element_type=F32)


def kernel(
    query, basis_in, basis_out, eig_in, eig_out, trace_in, trace_grad, out,
    b_in, b_out, gathered, rot_in_f, rot_out_f, rot_in, rot_out, traces, own,
    sib_recv, ring_send, ring_recv, pair, pair_recv,
    load_sem, q_send, q_recv, qs_send, qs_recv, t_send, t_recv,
    s_send, s_recv, r_send, r_recv, g_send, g_recv, p_send, p_recv,
):
    me = lax.axis_index("basis")
    core = lax.rem(me, 2)
    other = 1 - core
    chip = me // 2
    depth = CHIPS // 2
    pos = jnp.where(lax.rem(chip, 2) == 0, chip // 2, CHIPS - 1 - chip // 2)

    def at(offset):
        return lax.rem(pos + offset + CHIPS, CHIPS)

    def device(place, which):
        spot = jnp.where(place < depth, 2 * place, 2 * (CHIPS - 1 - place) + 1)
        return spot * 2 + which

    sibling = device(pos, other)
    ahead, behind = device(at(1), core), device(at(-1), core)
    toward = (ahead, behind)

    local = [
        pltpu.make_async_copy(basis_in, b_in, load_sem.at[0]),
        pltpu.make_async_copy(basis_out, b_out, load_sem.at[1]),
    ]
    mine = pl.ds(pl.multiple_of(me * PAD, PAD), PAD)
    first = pltpu.make_async_copy(query, gathered.at[mine], load_sem.at[4])
    first.start()

    barrier = pltpu.get_barrier_semaphore()
    for partner in (sibling, ahead, behind):
        pl.semaphore_signal(
            barrier, inc=1, device_id={"basis": partner}, device_id_type=pl.DeviceIdType.MESH
        )
    pl.semaphore_wait(barrier, 3)

    def remote(src, dst, send, recv, target):
        return pltpu.make_async_remote_copy(
            src_ref=src, dst_ref=dst, send_sem=send, recv_sem=recv,
            device_id={"basis": target}, device_id_type=pl.DeviceIdType.MESH,
        )

    first.wait()

    def block(owner, piece):
        rows = pl.ds(pl.multiple_of(owner * PAD, PAD), PAD)
        return gathered.at[rows, pl.ds(piece * HALF, HALF)]

    def hop(way, step, piece):
        owner = device(at(-step if way == 0 else step), core)
        ref = block(owner, piece)
        return remote(
            ref, ref, q_send.at[way, step, piece], q_recv.at[way, step, piece], toward[way]
        )

    def share(slot, place, piece):
        ref = block(device(place, core), piece)
        return remote(ref, ref, qs_send.at[slot, piece], qs_recv.at[slot, piece], sibling)

    q_copies, s_copies = [], []

    def send_query(way, step, piece):
        if step == HOPS - 1 and piece != way:
            return
        copy = hop(way, step, piece)
        copy.start()
        q_copies.append(copy)

    def send_share(slot, place, piece):
        copy = share(slot, place, piece)
        copy.start()
        s_copies.append(copy)

    for piece in range(2):
        for way in range(2):
            send_query(way, 0, (piece + way) % 2)
    for piece in range(2):
        send_share(0, pos, piece)
    for copy in local:
        copy.start()

    def trace_parts(which, target_rows):
        in_from = pl.ds(pl.multiple_of(which * IN_HALF, 128), IN_HALF)
        out_from = pl.ds(pl.multiple_of(which * OUT_HALF, 128), OUT_HALF)
        return (
            (trace_in.at[:, in_from], traces.at[target_rows, pl.ds(0, IN_HALF)]),
            (trace_grad.at[:, out_from], traces.at[target_rows, pl.ds(IN_HALF, OUT_HALF)]),
        )

    local_rows = trace_in.shape[0]
    t_rows = pl.ds(pl.multiple_of(core * local_rows, local_rows), local_rows)
    keep = [
        pltpu.make_async_copy(src, dst, load_sem.at[2 + i])
        for i, (src, dst) in enumerate(trace_parts(core, t_rows))
    ]
    give = [
        remote(src, dst, t_send.at[i], t_recv.at[i], sibling)
        for i, (src, dst) in enumerate(trace_parts(other, t_rows))
    ]

    for step in range(HOPS):
        for piece in range(2):
            for way in range(2):
                part = (piece + way) % 2
                if step == HOPS - 1 and part != way:
                    continue
                hop(way, step, part).wait_recv()
                if step < HOPS - 1:
                    send_query(way, step + 1, part)
                place = at(-1 - step if way == 0 else 1 + step)
                if step == HOPS - 1:
                    send_share(2 * HOPS - 1, place, part)
                else:
                    send_share(1 + 2 * step + way, place, part)
        if step == 0:
            for copy in keep + give:
                copy.start()
    for copy in local:
        copy.wait()
    for copy in s_copies:
        copy.wait()
    for copy in q_copies:
        copy.wait_send()

    rot_in_f[...] = jnp.zeros_like(rot_in_f)
    rot_out_f[...] = jnp.zeros_like(rot_out_f)

    @pl.loop(0, DA // KTILE)
    def _(k):
        start = pl.multiple_of(k * KTILE, KTILE)
        rot_in_f[...] += jnp.dot(
            gathered[:, pl.ds(start, KTILE)], b_in[pl.ds(start, KTILE), :],
            preferred_element_type=F32,
        )

    @pl.loop(0, FW // KTILE)
    def _(k):
        start = pl.multiple_of(k * KTILE, KTILE)
        rot_out_f[...] += jnp.dot(
            gathered[:, pl.ds(start + DA, KTILE)], b_out[pl.ds(start, KTILE), :],
            preferred_element_type=F32,
        )

    for total, eig, rot in ((rot_in_f, eig_in, rot_in), (rot_out_f, eig_out, rot_out)):
        scale = eig[...] + damping
        for i in range(CHIPS * CORES):
            total[pl.ds(i * ROWS, ROWS), :] = total[pl.ds(i * PAD, ROWS), :] / scale
        rot[...] = total[pl.ds(0, QROWS), :].astype(BF16)

    order = [HOPS]
    for d in range(HOPS - 1, 0, -1):
        order += [d, -d]
    order += [0]

    def in_rows(which, place):
        return pl.ds(pl.multiple_of(which * IN_HALF + place * IN_CHUNK, 128), IN_CHUNK)

    def out_rows(which, place):
        return pl.ds(pl.multiple_of(which * OUT_HALF + place * OUT_CHUNK, 128), OUT_CHUNK)

    def stage(j):
        return gathered.at[pl.ds(0, QROWS), pl.ds(HALF + j * CHUNK, CHUNK)]

    sib = []

    def compute(j):
        place = at(order[j])
        stage(j)[:, :IN_CHUNK] = nt(rot_in[...], b_in[in_rows(other, place), :]).astype(BF16)
        stage(j)[:, IN_CHUNK:] = nt(rot_out[...], b_out[out_rows(other, place), :]).astype(BF16)
        copy = remote(stage(j), sib_recv.at[j], s_send.at[j], s_recv.at[j], sibling)
        copy.start()
        sib.append(copy)
        own[j % 3, :, :IN_CHUNK] = nt(rot_in[...], b_in[in_rows(core, place), :])
        own[j % 3, :, IN_CHUNK:] = nt(rot_out[...], b_out[out_rows(core, place), :])

    ring = {}

    def ring_copy(way, step):
        if step == 0:
            rows = pl.ds(way * (QROWS // 2), QROWS // 2)
            src, dst = ring_send.at[way, step, rows], ring_recv.at[way, step, rows]
        else:
            src, dst = ring_send.at[way, step], ring_recv.at[way, step]
        return remote(src, dst, r_send.at[way, step], r_recv.at[way, step], toward[way])

    halves = (pl.ds(0, QROWS // 2), pl.ds(QROWS // 2, QROWS // 2))
    compute(0)
    compute(1)
    compute(2)
    sib[0].wait_recv()
    for way in range(2):
        rows = halves[way]
        ring_send[way, 0, rows] = (own[0, rows] + sib_recv[0, rows].astype(F32)).astype(BF16)
        ring[way, 0] = ring_copy(way, 0)
        ring[way, 0].start()
    for step in range(1, HOPS):
        for way in range(2):
            j = 1 + 2 * (step - 1) + way
            sib[j].wait_recv()
            ring[way, step - 1].wait_recv()
            if step == 1:
                a, b = halves[way], halves[1 - way]
                ring_send[way, 1, a] = (
                    own[j % 3, a] + sib_recv[j, a].astype(F32) + ring_recv[way, 0, a].astype(F32)
                ).astype(BF16)
                ring_send[way, 1, b] = (own[j % 3, b] + sib_recv[j, b].astype(F32)).astype(BF16)
            else:
                ring_send[way, step] = (
                    own[j % 3] + sib_recv[j].astype(F32) + ring_recv[way, step - 1].astype(F32)
                ).astype(BF16)
            ring[way, step] = ring_copy(way, step)
            ring[way, step].start()
        if step < HOPS - 1:
            compute(2 * step + 1)
            compute(2 * step + 2)
        else:
            compute(2 * HOPS - 1)
    last = 2 * HOPS - 1
    sib[last].wait_recv()
    for way in range(2):
        ring[way, HOPS - 1].wait_recv()

    def chunk(place):
        cols = pl.ds(pl.multiple_of(place * CHUNK, 128), CHUNK)
        return gathered.at[pl.ds(0, QROWS), cols]

    chunk(pos)[...] = (
        own[last % 3] + sib_recv[last].astype(F32)
        + ring_recv[0, HOPS - 1].astype(F32) + ring_recv[1, HOPS - 1].astype(F32)
    ).astype(BF16)

    spread = {}

    def spread_copy(way, step):
        place = at(-step if way == 0 else step)
        if step == HOPS - 1:
            rows = halves[way]
            cols = pl.ds(pl.multiple_of(place * CHUNK, 128), CHUNK)
            ref = gathered.at[rows, cols]
        else:
            ref = chunk(place)
        return remote(ref, ref, g_send.at[way, step], g_recv.at[way, step], toward[way])

    for way in range(2):
        spread[way, 0] = spread_copy(way, 0)
        spread[way, 0].start()
    for copy in keep:
        copy.wait()
    for copy in give:
        copy.wait()

    def multiply(place):
        block_of = chunk(place)
        t_in = pl.ds(pl.multiple_of(place * IN_CHUNK, 128), IN_CHUNK)
        t_out = pl.ds(pl.multiple_of(IN_HALF + place * OUT_CHUNK, 128), OUT_CHUNK)
        return (
            nt(traces[:, t_in], block_of[:, :IN_CHUNK]),
            nt(traces[:, t_out], block_of[:, IN_CHUNK:]),
        )

    pair[0], pair[1] = multiply(pos)
    for step in range(HOPS):
        for way in range(2):
            spread[way, step].wait_recv()
            if step < HOPS - 1:
                spread[way, step + 1] = spread_copy(way, step + 1)
                spread[way, step + 1].start()
        for way in range(2 if step < HOPS - 1 else 1):
            a, b = multiply(at(-1 - step if way == 0 else 1 + step))
            pair[0] += a
            pair[1] += b

    their_rows = pl.ds(pl.multiple_of(other * local_rows, local_rows), local_rows)
    swap = remote(pair.at[:, their_rows], pair_recv, p_send, p_recv, sibling)
    swap.start()
    swap.wait_recv()
    left = pair[0, t_rows, :] + pair_recv[0]
    right = pair[1, t_rows, :] + pair_recv[1]
    traces_here = local_rows // TTOK
    products = left * right
    sums = jnp.concatenate(
        [
            jnp.sum(products[i * TTOK : (i + 1) * TTOK], axis=0, keepdims=True)
            for i in range(traces_here)
        ],
        axis=0,
    )
    query_of = lax.broadcasted_iota(jnp.int32, (QUERIES, QROWS), 0) * QTOK
    token = lax.broadcasted_iota(jnp.int32, (QUERIES, QROWS), 1)
    select = jnp.where((token >= query_of) & (token < query_of + QTOK), 1.0, 0.0).astype(F32)
    scores = lax.dot_general(
        select, sums, (((1,), (1,)), ((), ())),
        precision=lax.Precision.HIGHEST, preferred_element_type=F32,
    )
    out[...] = scores * (1.0 / (math.sqrt(DA) * math.sqrt(FW) * TTOK * QTOK))

    swap.wait_send()
    for copy in sib:
        copy.wait_send()
    for copy in list(ring.values()) + list(spread.values()):
        copy.wait_send()


def per_device_ring(
    query_inputs, query_grads, basis_in, basis_out, eig_in, eig_out, trace_inputs, trace_grads
):
    query = jnp.pad(
        jnp.concatenate([query_inputs, query_grads], axis=1), ((0, PAD - ROWS), (0, 0))
    )
    cin, cout = basis_in.shape[1], basis_out.shape[1]
    rows = trace_inputs.shape[0]
    dma = pltpu.SemaphoreType.DMA
    padded = CHIPS * CORES * PAD
    vmem = pl.BlockSpec(memory_space=pltpu.VMEM)
    hbm = pl.BlockSpec(memory_space=pl.ANY)
    return pl.pallas_call(
        kernel,
        out_shape=jax.ShapeDtypeStruct((QUERIES, rows // TTOK), F32),
        in_specs=[hbm, hbm, hbm, vmem, vmem, hbm, hbm],
        out_specs=vmem,
        scratch_shapes=[
            pltpu.VMEM((DA, cin), BF16),
            pltpu.VMEM((FW, cout), BF16),
            pltpu.VMEM((padded, FEAT), BF16),
            pltpu.VMEM((padded, cin), F32),
            pltpu.VMEM((padded, cout), F32),
            pltpu.VMEM((QROWS, cin), BF16),
            pltpu.VMEM((QROWS, cout), BF16),
            pltpu.VMEM((CORES * rows, HALF), BF16),
            pltpu.VMEM((3, QROWS, CHUNK), F32),
            pltpu.VMEM((2 * HOPS, QROWS, CHUNK), BF16),
            pltpu.VMEM((2, HOPS, QROWS, CHUNK), BF16),
            pltpu.VMEM((2, HOPS, QROWS, CHUNK), BF16),
            pltpu.VMEM((2, CORES * rows, QROWS), F32),
            pltpu.VMEM((2, rows, QROWS), F32),
            dma((5,)),
            dma((2, HOPS, 2)),
            dma((2, HOPS, 2)),
            dma((2 * HOPS, 2)),
            dma((2 * HOPS, 2)),
            dma((2,)),
            dma((2,)),
            dma((2 * HOPS,)),
            dma((2 * HOPS,)),
            dma((2, HOPS)),
            dma((2, HOPS)),
            dma((2, HOPS)),
            dma((2, HOPS)),
            dma(()),
            dma(()),
        ],
        compiler_params=pltpu.CompilerParams(
            collective_id=0, has_side_effects=True, vmem_limit_bytes=63 * 1024 * 1024
        ),
        name="influence",
    )(
        query, basis_in, basis_out, eig_in.reshape(1, cin), eig_out.reshape(1, cout),
        trace_inputs, trace_grads,
    )


def per_device_plain(
    query_inputs, query_grads, basis_in, basis_out, eig_in, eig_out, trace_inputs, trace_grads
):
    def gather(x):
        return lax.all_gather(x, "basis", axis=0, tiled=True)

    def condition(query, basis, eig):
        rot = (jnp.dot(gather(query), basis, preferred_element_type=F32) / (eig + damping)).astype(
            BF16
        )
        share = lax.psum_scatter(
            jnp.dot(basis, rot.T, preferred_element_type=F32),
            "basis",
            scatter_dimension=0,
            tiled=True,
        )
        return gather(share.astype(BF16)).astype(F32)

    pre_in = condition(query_inputs, basis_in, eig_in)
    pre_grad = condition(query_grads, basis_out, eig_out)
    high = lax.Precision.HIGHEST
    pair_in = jnp.dot(trace_inputs.astype(F32), pre_in, precision=high) / math.sqrt(DA)
    pair_grad = jnp.dot(trace_grads.astype(F32), pre_grad, precision=high) / math.sqrt(FW)
    local_traces = trace_inputs.shape[0] // TTOK
    products = (pair_in * pair_grad).reshape(local_traces, TTOK, QUERIES, QTOK)
    return jnp.sum(products, axis=(1, 3)).T / (TTOK * QTOK)


def solution(mesh):
    fits = mesh.shape["basis"] == CHIPS * CORES
    return jax.shard_map(
        per_device_ring if fits else per_device_plain,
        mesh=mesh,
        in_specs=(
            P(("grp", "basis"), None),
            P(("grp", "basis"), None),
            P(None, "basis"),
            P(None, "basis"),
            P("basis"),
            P("basis"),
            P(("grp", "basis"), None),
            P(("grp", "basis"), None),
        ),
        out_specs=P(None, ("grp", "basis")),
        check_vma=False,
    )
```

time: 431 us -> 151 us (0.35)
  waiting for transfers between devices: 356 us -> 0 us
  Pallas kernels: 0 us -> 146 us
  matrix products: 42.5 us -> 0 us
  between operations: 13.5 us -> 0.01 us
  local copies, waits for them, and re-layouts: 12.7 us -> 2.66 us
    all_gather x4 -> x0, waiting for transfers between devices: 201 us -> none  [the longest x1 60.7 us: per_device(): lax.all_gather(query_grads, 'basis', axis=0, tiled=True)]
    reduce_scatter x2 -> x0, waiting for transfers between devices: 153 us -> none  [the longest x1 125 us: per_device(): lax.psum_scatter(jnp.dot(block, rot_grad.T, preferred_element_type=jnp.fl...]
    pallas_call x0 -> x1, Pallas kernels: none -> 146 us  [per_device_ring(): pl.pallas_call(kernel, out_shape=jax.ShapeDtypeStruct((QUERIES, rows // T...]
    dot_general x5 -> x0, matrix products: 42.5 us -> none  [the longest x1 15.9 us: per_device(): jnp.dot(block, rot_grad.T, preferred_element_type=jnp.float32)]
    unnamed x8 -> x0, local copies, waits for them, and re-layouts: 11.9 us -> none
  transfers between devices with their start and end apart: 6 -> 0, of which waited for: 6 -> 0; matrix products, arithmetic and copies ran while one was open for 13% -> 0% of each run, Pallas kernels for 0% -> 0%
where the time goes in v1:
time: 151 us; the launch traced here: 150 us
  Pallas kernels  146 us (97%)
  local copies, waits for them, and re-layouts  2.66 us (2%)
  other arithmetic  1.94 us (1%)
    pallas_call x1, Pallas kernels, per_device_ring(): pl.pallas_call(kernel, out_shape=jax.ShapeDtypeStruct((QUERIES, rows // T...  146 us

profile of v1, /device:TPU:1, one launch (start us, length us, event | category | flops | bytes accessed | tf_op | source)
XLA Modules:
  0.0 150.5 jit_solution(9965395609471350629)
XLA Ops:
  0.0 1.3 reshape.7.eig_out
  1.3 1.9 %fusion.2.query = bf16[16,18432]{1,0:T(8,128)(2,1)} fusion(bf16[12,14336]{1,0:T(8,128)(2,1)} %param.9, bf16[12,4096]{1,0:T(8,128)(2,1)} %param.8), kind=kLoop, calls=%fused_computation.3 | loop fusion | flops 2064384 | bytes 1032192 | tf_op jit(solution)/shard_map/concatenate | solution.py:349
  3.2 145.9 %influence.1 = f32[64,2]{1,0:T(8,128)} custom-call(bf16[16,18432]{1,0:T(8,128)(2,1)} %fusion.2.query, bf16[4096,256]{1,0:T(8,128)(2,1)} %basis_in.1, bf16[14336,896]{1,0:T(8,128)(2,1)} %basis_out.1, f32[1,256]{1,0:T(1,128)} %bitcast.1, f32[1,896]{1,0:T(1,128)} %reshape.7.eig_out, bf16[128,4096]{1,0:T(8,128)(2,1)} %trace_in.1, bf16[128,14336]{1,0:T(8,128)(2,1)} %trace_grad.1), custom_call_target="tpu_custom_call" | custom-call | tf_op jit(solution)/shard_map/influence/pallas_call | solution.py:357
  149.1 1.4 copy.9

commit v2 on v1

--- a/solution.py
+++ b/solution.py
@@ -25,6 +25,13 @@
 IN_CHUNK, OUT_CHUNK = IN_HALF // CHIPS, OUT_HALF // CHIPS
 CHUNK = IN_CHUNK + OUT_CHUNK
 KTILE = 1024
+GROUPS = 3
+SPARE = PAD - ROWS
+EXTRA = FEAT // (GROUPS + 1)
+WIDE = FEAT - EXTRA
+PARTS = ((0, GROUPS - 1), (GROUPS - 1, GROUPS))
+TAIL = FW - EXTRA
+ETILE = EXTRA // 3
 
 damping = 0.1
 F32 = jnp.float32
@@ -37,7 +44,8 @@
 
 def kernel(
     query, basis_in, basis_out, eig_in, eig_out, trace_in, trace_grad, out,
-    b_in, b_out, gathered, rot_in_f, rot_out_f, rot_in, rot_out, traces, own,
+    b_in, b_out, gathered, extra, lifted, rot_in_f, rot_out_f, rot_extra, rot_in, rot_out,
+    traces, own,
     sib_recv, ring_send, ring_recv, pair, pair_recv,
     load_sem, q_send, q_recv, qs_send, qs_recv, t_send, t_recv,
     s_send, s_recv, r_send, r_recv, g_send, g_recv, p_send, p_recv,
@@ -83,40 +91,54 @@
 
     first.wait()
 
-    def block(owner, piece):
+    def block(owner, part, piece):
         rows = pl.ds(pl.multiple_of(owner * PAD, PAD), PAD)
-        return gathered.at[rows, pl.ds(piece * HALF, HALF)]
-
-    def hop(way, step, piece):
+        low, high = PARTS[part]
+        width = (high - low) * EXTRA // 2
+        return gathered.at[rows, pl.ds(low * EXTRA + piece * width, width)]
+
+    def hop(part, way, step, piece):
         owner = device(at(-step if way == 0 else step), core)
-        ref = block(owner, piece)
-        return remote(
-            ref, ref, q_send.at[way, step, piece], q_recv.at[way, step, piece], toward[way]
-        )
-
-    def share(slot, place, piece):
-        ref = block(device(place, core), piece)
-        return remote(ref, ref, qs_send.at[slot, piece], qs_recv.at[slot, piece], sibling)
-
-    q_copies, s_copies = [], []
-
-    def send_query(way, step, piece):
+        ref = block(owner, part, piece)
+        sems = q_send.at[part, way, step, piece], q_recv.at[part, way, step, piece]
+        return remote(ref, ref, *sems, toward[way])
+
+    q_copies, s_copies = [], ([], [])
+
+    def send_query(part, way, step, piece):
         if step == HOPS - 1 and piece != way:
             return
-        copy = hop(way, step, piece)
+        copy = hop(part, way, step, piece)
         copy.start()
         q_copies.append(copy)
 
-    def send_share(slot, place, piece):
-        copy = share(slot, place, piece)
+    def send_share(part, slot, place, piece):
+        ref = block(device(place, core), part, piece)
+        sems = qs_send.at[part, slot, piece], qs_recv.at[part, slot, piece]
+        copy = remote(ref, ref, *sems, sibling)
         copy.start()
-        s_copies.append(copy)
-
-    for piece in range(2):
+        s_copies[part].append(copy)
+
+    def open_part(part):
+        for piece in range(2):
+            for way in range(2):
+                send_query(part, way, 0, (piece + way) % 2)
+        for piece in range(2):
+            send_share(part, 0, pos, piece)
+
+    def pass_on(part, step, turn):
         for way in range(2):
-            send_query(way, 0, (piece + way) % 2)
-    for piece in range(2):
-        send_share(0, pos, piece)
+            piece = (turn + way) % 2
+            if step == HOPS - 1 and piece != way:
+                continue
+            hop(part, way, step, piece).wait_recv()
+            if step < HOPS - 1:
+                send_query(part, way, step + 1, piece)
+            place = at(-1 - step if way == 0 else 1 + step)
+            slot = 2 * HOPS - 1 if step == HOPS - 1 else 1 + 2 * step + way
+            send_share(part, slot, place, piece)
+
+    open_part(0)
     for copy in local:
         copy.start()
 
@@ -139,54 +161,89 @@
         for i, (src, dst) in enumerate(trace_parts(other, t_rows))
     ]
 
-    for step in range(HOPS):
-        for piece in range(2):
-            for way in range(2):
-                part = (piece + way) % 2
-                if step == HOPS - 1 and part != way:
-                    continue
-                hop(way, step, part).wait_recv()
-                if step < HOPS - 1:
-                    send_query(way, step + 1, part)
-                place = at(-1 - step if way == 0 else 1 + step)
-                if step == HOPS - 1:
-                    send_share(2 * HOPS - 1, place, part)
-                else:
-                    send_share(1 + 2 * step + way, place, part)
-        if step == 0:
+    rounds = [(step, turn) for step in range(HOPS) for turn in range(2)][: 2 * HOPS - 1]
+    for i, (step, turn) in enumerate(rounds):
+        if i == len(rounds) - 1:
+            open_part(1)
+        pass_on(0, step, turn)
+        if i == 1:
             for copy in keep + give:
                 copy.start()
-    for copy in local:
+
+    def add_in(start):
+        rot_in_f[...] += jnp.dot(
+            gathered[:, start : start + KTILE], b_in[start : start + KTILE, :],
+            preferred_element_type=F32,
+        )
+
+    def add_out(start, size):
+        rot_out_f[...] += jnp.dot(
+            gathered[:, start + DA : start + DA + size], b_out[start : start + size, :],
+            preferred_element_type=F32,
+        )
+
+    def lift(group):
+        cols = pl.ds(group * EXTRA, EXTRA)
+        per_tile = PAD // SPARE
+        tiles = CHIPS * CORES // per_tile
+        for tile in range(tiles):
+            for i in range(per_tile):
+                rows = pl.ds((tile * per_tile + i) * PAD, PAD)
+                lifted[pl.ds(i * SPARE, SPARE), :] = gathered[rows, cols].astype(F32)[ROWS:]
+            extra[pl.ds((group * tiles + tile) * PAD, PAD), :] = lifted[...].astype(BF16)
+
+    block_rows = CHIPS * CORES * SPARE
+
+    def add_extra(part, start):
+        low, high = PARTS[part]
+        rows = pl.ds(low * block_rows, (high - low) * block_rows)
+        rot_extra[rows, :] += jnp.dot(
+            extra[rows, start : start + ETILE],
+            b_out[TAIL + start : TAIL + start + ETILE, :],
+            preferred_element_type=F32,
+        )
+
+    early = PARTS[0][1] * EXTRA - DA
+    rot_in_f[...] = jnp.zeros_like(rot_in_f)
+    rot_out_f[...] = jnp.zeros_like(rot_out_f)
+    rot_extra[...] = jnp.zeros_like(rot_extra)
+    jobs = [functools.partial(add_in, k) for k in range(0, DA, KTILE)]
+    jobs += [functools.partial(add_out, k, KTILE) for k in range(0, early, KTILE)]
+    jobs += [functools.partial(lift, g) for g in range(*PARTS[0])]
+    jobs += [functools.partial(add_extra, 0, k) for k in range(0, EXTRA, ETILE)]
+    share_out = -(-len(jobs) // (len(rounds) - 1))
+    for i, (step, turn) in enumerate(rounds):
+        pass_on(1, step, turn)
+        if i == 0:
+            for copy in local:
+                copy.wait()
+            for copy in s_copies[0]:
+                copy.wait()
+        for job in jobs[i * share_out : (i + 1) * share_out]:
+            job()
+    for copy in s_copies[1]:
         copy.wait()
-    for copy in s_copies:
-        copy.wait()
+    for group in range(*PARTS[1]):
+        lift(group)
+    for k in range(early, TAIL, ETILE):
+        add_out(k, ETILE)
+    for k in range(0, EXTRA, ETILE):
+        add_extra(1, k)
     for copy in q_copies:
         copy.wait_send()
 
-    rot_in_f[...] = jnp.zeros_like(rot_in_f)
-    rot_out_f[...] = jnp.zeros_like(rot_out_f)
-
-    @pl.loop(0, DA // KTILE)
-    def _(k):
-        start = pl.multiple_of(k * KTILE, KTILE)
-        rot_in_f[...] += jnp.dot(
-            gathered[:, pl.ds(start, KTILE)], b_in[pl.ds(start, KTILE), :],
-            preferred_element_type=F32,
-        )
-
-    @pl.loop(0, FW // KTILE)
-    def _(k):
-        start = pl.multiple_of(k * KTILE, KTILE)
-        rot_out_f[...] += jnp.dot(
-            gathered[:, pl.ds(start + DA, KTILE)], b_out[pl.ds(start, KTILE), :],
-            preferred_element_type=F32,
-        )
-
-    for total, eig, rot in ((rot_in_f, eig_in, rot_in), (rot_out_f, eig_out, rot_out)):
-        scale = eig[...] + damping
-        for i in range(CHIPS * CORES):
-            total[pl.ds(i * ROWS, ROWS), :] = total[pl.ds(i * PAD, ROWS), :] / scale
-        rot[...] = total[pl.ds(0, QROWS), :].astype(BF16)
+    scale = eig_in[...] + damping
+    for i in range(CHIPS * CORES):
+        rot_in_f[pl.ds(i * ROWS, ROWS), :] = rot_in_f[pl.ds(i * PAD, ROWS), :] / scale
+    rot_in[...] = rot_in_f[pl.ds(0, QROWS), :].astype(BF16)
+    scale = eig_out[...] + damping
+    for i in range(CHIPS * CORES):
+        for group in range(GROUPS):
+            rot_out_f[pl.ds(i * ROWS + group * SPARE, SPARE), :] = (
+                rot_out_f[pl.ds(i * PAD + group * SPARE, SPARE), :]
+                + rot_extra[pl.ds(group * block_rows + i * SPARE, SPARE), :]
+            ) / scale
+    rot_out[...] = rot_out_f[pl.ds(0, QROWS), :].astype(BF16)
 
     order = [HOPS]
     for d in range(HOPS - 1, 0, -1):
@@ -200,7 +257,10 @@
         return pl.ds(pl.multiple_of(which * OUT_HALF + place * OUT_CHUNK, 128), OUT_CHUNK)
 
     def stage(j):
-        return gathered.at[pl.ds(0, QROWS), pl.ds(HALF + j * CHUNK, CHUNK)]
+        spots = (WIDE - HALF) // CHUNK
+        if j < spots:
+            return gathered.at[pl.ds(0, QROWS), pl.ds(HALF + j * CHUNK, CHUNK)]
+        return extra.at[:, pl.ds((j - spots) * CHUNK, CHUNK)]
 
     sib = []
 
@@ -215,76 +275,74 @@
         own[j % 3, :, IN_CHUNK:] = nt(rot_out[...], b_out[out_rows(core, place), :])
 
     ring = {}
-
-    def ring_copy(way, step):
-        if step == 0:
-            rows = pl.ds(way * (QROWS // 2), QROWS // 2)
-            src, dst = ring_send.at[way, step, rows], ring_recv.at[way, step, rows]
-        else:
-            src, dst = ring_send.at[way, step], ring_recv.at[way, step]
-        return remote(src, dst, r_send.at[way, step], r_recv.at[way, step], toward[way])
-
     halves = (pl.ds(0, QROWS // 2), pl.ds(QROWS // 2, QROWS // 2))
+
+    def send_sum(step, far):
+        for way in range(2):
+            half = way if far else 1 - way
+            rows = halves[half]
+            j = 0 if step == 0 else 2 * step - 1 + way
+            if ("sib", j) not in seen:
+                sib[j].wait_recv()
+                seen.add(("sib", j))
+            total = own[j % 3, rows] + sib_recv[j, rows].astype(F32)
+            if (way, step - 1, half) in ring:
+                ring[way, step - 1, half].wait_recv()
+                total = total + ring_recv[way, step - 1, rows].astype(F32)
+            ring_send[way, step, rows] = total.astype(BF16)
+            copy = remote(
+                ring_send.at[way, step, rows], ring_recv.at[way, step, rows],
+                r_send.at[way, step, half], r_recv.at[way, step, half], toward[way],
+            )
+            copy.start()
+            ring[way, step, half] = copy
+
+    seen = set()
     compute(0)
+    send_sum(0, True)
     compute(1)
     compute(2)
-    sib[0].wait_recv()
-    for way in range(2):
-        rows = halves[way]
-        ring_send[way, 0, rows] = (own[0, rows] + sib_recv[0, rows].astype(F32)).astype(BF16)
-        ring[way, 0] = ring_copy(way, 0)
-        ring[way, 0].start()
     for step in range(1, HOPS):
-        for way in range(2):
-            j = 1 + 2 * (step - 1) + way
-            sib[j].wait_recv()
-            ring[way, step - 1].wait_recv()
-            if step == 1:
-                a, b = halves[way], halves[1 - way]
-                ring_send[way, 1, a] = (
-                    own[j % 3, a] + sib_recv[j, a].astype(F32) + ring_recv[way, 0, a].astype(F32)
-                ).astype(BF16)
-                ring_send[way, 1, b] = (own[j % 3, b] + sib_recv[j, b].astype(F32)).astype(BF16)
-            else:
-                ring_send[way, step] = (
-                    own[j % 3] + sib_recv[j].astype(F32) + ring_recv[way, step - 1].astype(F32)
-                ).astype(BF16)
-            ring[way, step] = ring_copy(way, step)
-            ring[way, step].start()
+        send_sum(step, False)
+        compute(2 * step + 1)
+        send_sum(step, True)
         if step < HOPS - 1:
-            compute(2 * step + 1)
             compute(2 * step + 2)
-        else:
-            compute(2 * HOPS - 1)
     last = 2 * HOPS - 1
     sib[last].wait_recv()
-    for way in range(2):
-        ring[way, HOPS - 1].wait_recv()
 
     def chunk(place):
         cols = pl.ds(pl.multiple_of(place * CHUNK, 128), CHUNK)
         return gathered.at[pl.ds(0, QROWS), cols]
 
-    chunk(pos)[...] = (
-        own[last % 3] + sib_recv[last].astype(F32)
-        + ring_recv[0, HOPS - 1].astype(F32) + ring_recv[1, HOPS - 1].astype(F32)
-    ).astype(BF16)
-
     spread = {}
 
-    def spread_copy(way, step):
-        place = at(-step if way == 0 else step)
-        if step == HOPS - 1:
-            rows = halves[way]
-            cols = pl.ds(pl.multiple_of(place * CHUNK, 128), CHUNK)
-            ref = gathered.at[rows, cols]
-        else:
-            ref = chunk(place)
-        return remote(ref, ref, g_send.at[way, step], g_recv.at[way, step], toward[way])
-
-    for way in range(2):
-        spread[way, 0] = spread_copy(way, 0)
-        spread[way, 0].start()
+    def part_of(place, half):
+        cols = pl.ds(pl.multiple_of(place * CHUNK, 128), CHUNK)
+        return gathered.at[halves[half], cols]
+
+    def send_spread(way, step, half):
+        if step == HOPS - 1 and half != way:
+            return
+        ref = part_of(at(-step if way == 0 else step), half)
+        sems = g_send.at[way, step, half], g_recv.at[way, step, half]
+        copy = remote(ref, ref, *sems, toward[way])
+        copy.start()
+        spread[way, step, half] = copy
+
+    for half in (1, 0):
+        ring[half ^ 1, HOPS - 1, half].wait_recv()
+    for half in range(2):
+        ring[half, HOPS - 1, half].wait_recv()
+        rows = halves[half]
+        part_of(pos, half)[...] = (
+            own[last % 3, rows] + sib_recv[last, rows].astype(F32)
+            + ring_recv[0, HOPS - 1, rows].astype(F32)
+            + ring_recv[1, HOPS - 1, rows].astype(F32)
+        ).astype(BF16)
+    for turn in range(2):
+        for way in range(2):
+            send_spread(way, 0, (turn + way) % 2)
     for copy in keep:
         copy.wait()
     for copy in give:
@@ -301,11 +359,13 @@
 
     pair[0], pair[1] = multiply(pos)
     for step in range(HOPS):
-        for way in range(2):
-            spread[way, step].wait_recv()
-            if step < HOPS - 1:
-                spread[way, step + 1] = spread_copy(way, step + 1)
-                spread[way, step + 1].start()
+        for turn in range(2):
+            for way in range(2):
+                half = (turn + way) % 2
+                if (way, step, half) in spread:
+                    spread[way, step, half].wait_recv()
+                    if step < HOPS - 1:
+                        send_spread(way, step + 1, half)
         for way in range(2 if step < HOPS - 1 else 1):
             a, b = multiply(at(-1 - step if way == 0 else 1 + step))
             pair[0] += a
@@ -345,8 +405,13 @@
 def per_device_ring(
     query_inputs, query_grads, basis_in, basis_out, eig_in, eig_out, trace_inputs, trace_grads
 ):
-    query = jnp.pad(
-        jnp.concatenate([query_inputs, query_grads], axis=1), ((0, PAD - ROWS), (0, 0))
+    spare = query_grads[:, TAIL:].reshape(GROUPS, SPARE, EXTRA).swapaxes(0, 1)
+    query = jnp.concatenate(
+        [
+            jnp.concatenate([query_inputs, query_grads[:, :TAIL]], axis=1),
+            spare.reshape(SPARE, WIDE),
+        ],
+        axis=0,
     )
     cin, cout = basis_in.shape[1], basis_out.shape[1]
     rows = trace_inputs.shape[0]
@@ -362,9 +427,12 @@
         scratch_shapes=[
             pltpu.VMEM((DA, cin), BF16),
             pltpu.VMEM((FW, cout), BF16),
-            pltpu.VMEM((padded, FEAT), BF16),
+            pltpu.VMEM((padded, WIDE), BF16),
+            pltpu.VMEM((QROWS, EXTRA), BF16),
+            pltpu.VMEM((PAD, EXTRA), F32),
             pltpu.VMEM((padded, cin), F32),
             pltpu.VMEM((padded, cout), F32),
+            pltpu.VMEM((QROWS, cout), F32),
             pltpu.VMEM((QROWS, cin), BF16),
             pltpu.VMEM((QROWS, cout), BF16),
             pltpu.VMEM((CORES * rows, HALF), BF16),
@@ -375,18 +443,18 @@
             pltpu.VMEM((2, CORES * rows, QROWS), F32),
             pltpu.VMEM((2, rows, QROWS), F32),
             dma((5,)),
-            dma((2, HOPS, 2)),
-            dma((2, HOPS, 2)),
-            dma((2 * HOPS, 2)),
-            dma((2 * HOPS, 2)),
+            dma((2, 2, HOPS, 2)),
+            dma((2, 2, HOPS, 2)),
+            dma((2, 2 * HOPS, 2)),
+            dma((2, 2 * HOPS, 2)),
             dma((2,)),
             dma((2,)),
             dma((2 * HOPS,)),
             dma((2 * HOPS,)),
-            dma((2, HOPS)),
-            dma((2, HOPS)),
-            dma((2, HOPS)),
-            dma((2, HOPS)),
+            dma((2, HOPS, 2)),
+            dma((2, HOPS, 2)),
+            dma((2, HOPS, 2)),
+            dma((2, HOPS, 2)),
             dma(()),
             dma(()),
         ],

time: 151 us -> 132 us (0.87)
  Pallas kernels: 146 us -> 125 us
  local copies, waits for them, and re-layouts: 2.66 us -> 4.63 us
    pallas_call x1, Pallas kernels: 146 us -> 125 us  [per_device_ring(): pl.pallas_call(kernel, out_shape=jax.ShapeDtypeStruct((QUERIES, rows // T...]
    slice x0 -> x2, local copies, waits for them, and re-layouts: none -> 1.91 us  [the longest x1 0.99 us: per_device_ring(): query_grads[:, :TAIL]]
where the time goes in v2:
time: 132 us
  Pallas kernels  125 us (95%)
  local copies, waits for them, and re-layouts  4.63 us (4%)
  other arithmetic  1.79 us (1%)
    pallas_call x1, Pallas kernels, per_device_ring(): pl.pallas_call(kernel, out_shape=jax.ShapeDtypeStruct((QUERIES, rows // T...  125 us

profile of v2, /device:TPU:1, one launch (start us, length us, event | category | flops | bytes accessed | tf_op | source)
XLA Modules:
  0.0 131.8 jit_solution(7172262277557650549)
XLA Ops:
  0.0 1.0 slice.6
  1.0 0.9 slice.7
  2.0 1.8 %pad_maximum_fusion.query = bf16[16,13824]{1,0:T(8,128)(2,1)} fusion(bf16[4,13824]{1,0:T(4,128)(2,1)S(1)} %bitcast.4, bf16[12,9728]{1,0:T(8,128)(2,1)S(1)} %slice.6, bf16[12,4096]{1,0:T(8,128)(2,1)} %param.8), kind=kLoop, calls=%fused_computation | loop fusion | flops 1327104 | bytes 884736 | tf_op jit(solution)/shard_map/concatenate | solution.py:409
  3.8 1.3 reshape.15.eig_out
  5.0 125.4 %influence.1 = f32[64,2]{1,0:T(8,128)} custom-call(bf16[16,13824]{1,0:T(8,128)(2,1)} %pad_maximum_fusion.query, bf16[4096,256]{1,0:T(8,128)(2,1)} %basis_in.1, bf16[14336,896]{1,0:T(8,128)(2,1)} %basis_out.1, f32[1,256]{1,0:T(1,128)} %bitcast.5, f32[1,896]{1,0:T(1,128)} %reshape.15.eig_out, bf16[128,4096]{1,0:T(8,128)(2,1)} %trace_in.1, ...), custom_call_target="tpu_custom_call" | custom-call | tf_op jit(solution)/shard_map/influence/pallas_call | solution.py:422
  130.4 1.4 %copy.11 = f32[64,2]{0,1:T(2,128)} copy(f32[64,2]{1,0:T(8,128)} %influence.1) | data formatting | bytes 1024 | tf_op jit(solution)/shard_map/influence/pallas_call | solution.py:422
  (1 shorter events, 0.0 us)

commit v3 on v2

--- a/solution.py
+++ b/solution.py
@@ -32,6 +32,7 @@
 PARTS = ((0, GROUPS - 1), (GROUPS - 1, GROUPS))
 TAIL = FW - EXTRA
 ETILE = EXTRA // 3
+LEAD = 1
 
 damping = 0.1
 F32 = jnp.float32
@@ -89,19 +90,23 @@
             device_id={"basis": target}, device_id_type=pl.DeviceIdType.MESH,
         )
 
-    first.wait()
-
     def block(owner, part, piece):
         rows = pl.ds(pl.multiple_of(owner * PAD, PAD), PAD)
         low, high = PARTS[part]
         width = (high - low) * EXTRA // 2
         return gathered.at[rows, pl.ds(low * EXTRA + piece * width, width)]
 
+    def origin(part, piece):
+        low, high = PARTS[part]
+        width = (high - low) * EXTRA // 2
+        return query.at[:, pl.ds(low * EXTRA + piece * width, width)]
+
     def hop(part, way, step, piece):
         owner = device(at(-step if way == 0 else step), core)
         ref = block(owner, part, piece)
+        src = origin(part, piece) if step == 0 else ref
         sems = q_send.at[part, way, step, piece], q_recv.at[part, way, step, piece]
-        return remote(ref, ref, *sems, toward[way])
+        return remote(src, ref, *sems, toward[way])
 
     q_copies, s_copies = [], ([], [])
 
@@ -115,7 +120,8 @@
     def send_share(part, slot, place, piece):
         ref = block(device(place, core), part, piece)
         sems = qs_send.at[part, slot, piece], qs_recv.at[part, slot, piece]
-        copy = remote(ref, ref, *sems, sibling)
+        src = origin(part, piece) if slot == 0 else ref
+        copy = remote(src, ref, *sems, sibling)
         copy.start()
         s_copies[part].append(copy)
 
@@ -163,9 +169,11 @@
 
     rounds = [(step, turn) for step in range(HOPS) for turn in range(2)][: 2 * HOPS - 1]
     for i, (step, turn) in enumerate(rounds):
-        if i == len(rounds) - 1:
+        if i == len(rounds) - LEAD - 1:
             open_part(1)
         pass_on(0, step, turn)
+        if i >= len(rounds) - LEAD:
+            pass_on(1, *rounds[i - len(rounds) + LEAD])
         if i == 1:
             for copy in keep + give:
                 copy.start()
@@ -203,18 +211,27 @@
             preferred_element_type=F32,
         )
 
+    def finish_in():
+        scale = eig_in[...].reshape(1, -1) + damping
+        for i in range(CHIPS * CORES):
+            rot_in_f[pl.ds(i * ROWS, ROWS), :] = rot_in_f[pl.ds(i * PAD, ROWS), :] / scale
+        rot_in[...] = rot_in_f[pl.ds(0, QROWS), :].astype(BF16)
+
     early = PARTS[0][1] * EXTRA - DA
     rot_in_f[...] = jnp.zeros_like(rot_in_f)
     rot_out_f[...] = jnp.zeros_like(rot_out_f)
     rot_extra[...] = jnp.zeros_like(rot_extra)
     jobs = [functools.partial(add_in, k) for k in range(0, DA, KTILE)]
+    jobs += [finish_in]
     jobs += [functools.partial(add_out, k, KTILE) for k in range(0, early, KTILE)]
     jobs += [functools.partial(lift, g) for g in range(*PARTS[0])]
     jobs += [functools.partial(add_extra, 0, k) for k in range(0, EXTRA, ETILE)]
-    share_out = -(-len(jobs) // (len(rounds) - 1))
-    for i, (step, turn) in enumerate(rounds):
+    rest = rounds[LEAD:]
+    share_out = -(-len(jobs) // len(rest))
+    for i, (step, turn) in enumerate(rest):
         pass_on(1, step, turn)
         if i == 0:
+            first.wait()
             for copy in local:
                 copy.wait()
             for copy in s_copies[0]:
@@ -232,11 +249,7 @@
     for copy in q_copies:
         copy.wait_send()
 
-    scale = eig_in[...] + damping
-    for i in range(CHIPS * CORES):
-        rot_in_f[pl.ds(i * ROWS, ROWS), :] = rot_in_f[pl.ds(i * PAD, ROWS), :] / scale
-    rot_in[...] = rot_in_f[pl.ds(0, QROWS), :].astype(BF16)
-    scale = eig_out[...] + damping
+    scale = eig_out[...].reshape(1, -1) + damping
     for i in range(CHIPS * CORES):
         for group in range(GROUPS):
             rot_out_f[pl.ds(i * ROWS + group * SPARE, SPARE), :] = (
@@ -463,7 +476,7 @@
         ),
         name="influence",
     )(
-        query, basis_in, basis_out, eig_in.reshape(1, cin), eig_out.reshape(1, cout),
+        query, basis_in, basis_out, eig_in, eig_out,
         trace_inputs, trace_grads,
     )
 

time: 132 us -> 131 us (level)
  no operation moved by 1% of the time
where the time goes in v3:
time: 131 us
  Pallas kernels  126 us (96%)
  local copies, waits for them, and re-layouts  3.35 us (3%)
  other arithmetic  1.79 us (1%)
    pallas_call x1, Pallas kernels, per_device_ring(): pl.pallas_call(kernel, out_shape=jax.ShapeDtypeStruct((QUERIES, rows // T...  126 us

profile of v3, /device:TPU:1, one launch (start us, length us, event | category | flops | bytes accessed | tf_op | source)
XLA Modules:
  0.0 131.0 jit_solution(14121001760933502496)
XLA Ops:
  0.0 0.9 slice.7
  1.0 1.0 slice.6
  2.0 1.8 %pad_maximum_fusion.query = bf16[16,13824]{1,0:T(8,128)(2,1)} fusion(bf16[4,13824]{1,0:T(4,128)(2,1)S(1)} %bitcast.3, bf16[12,9728]{1,0:T(8,128)(2,1)S(1)} %slice.6, bf16[12,4096]{1,0:T(8,128)(2,1)} %param.8), kind=kLoop, calls=%fused_computation | loop fusion | flops 1327104 | bytes 884736 | tf_op jit(solution)/shard_map/concatenate | solution.py:422
  3.8 125.8 %influence.1 = f32[64,2]{1,0:T(8,128)} custom-call(bf16[16,13824]{1,0:T(8,128)(2,1)} %pad_maximum_fusion.query, bf16[4096,256]{1,0:T(8,128)(2,1)} %basis_in.1, bf16[14336,896]{1,0:T(8,128)(2,1)} %basis_out.1, f32[256]{0:T(256)} %eig_in.1, f32[896]{0:T(1024)} %eig_out.1, bf16[128,4096]{1,0:T(8,128)(2,1)} %trace_in.1, bf16[128,14336]{1,0:T(8,128)(2,1)} %trace_grad.1), custom_call_target="tpu_custom_call" | custom-call | tf_op jit(solution)/shard_map/influence/pallas_call | solution.py:435
  129.6 1.4 %copy.11 = f32[64,2]{0,1:T(2,128)} copy(f32[64,2]{1,0:T(8,128)} %influence.1) | data formatting | bytes 1024 | tf_op jit(solution)/shard_map/influence/pallas_call | solution.py:435
  (1 shorter events, 0.0 us)
